TPU v7x, 32 devices: a whole 2x2x4 slice. The times are simulated.
32 devices in a mesh: groups: 2 (over y), row: 4 (over x, core), col: 4 (over z).
Axes of the slice: x: 2, y: 2, z: 4, core: 2. Of those that a mesh axis runs over, the one named last changes fastest.
Arguments:
- features: bfloat16 [512, 256, 128], P(('groups', 'row'), 'col'), parts along dimension 0, may hold values from -6 to 6
- kernel_first: bfloat16 [3, 3, 128, 128], replicated, may hold values from -0.1875 to 0.1875
- bias_first: float32 [128], replicated, may hold values from -3 to 3
- mixer_first: bfloat16 [128, 128], replicated, may hold values from -0.5 to 0.5
- shift_first: float32 [128], replicated, may hold values from -3 to 3
- kernel_second: bfloat16 [3, 3, 128, 128], replicated, may hold values from -0.1875 to 0.1875
- bias_second: float32 [128], replicated, may hold values from -3 to 3
- mixer_second: bfloat16 [128, 128], replicated, may hold values from -0.5 to 0.5
- shift_second: float32 [128], replicated, may hold values from -3 to 3
Outputs:
- contacts: float32 [512, 256, 128], P(('groups', 'row'), 'col'), parts along dimension 0
There are 2 independent parts, one for each index of `groups`. A program takes and returns all parts, laid end to end along the dimension named above; an argument that names none is the same for every part. Nothing has to cross between parts.
All inputs are finite; a program needn't handle non-finite values.
Results may differ from a plain program's by a relative error of at most 0.0045.
Values may be sent and summed in bfloat16 or wider, within the bound.
A program may use at most 64 MiB of HBM per device.

v0:
```python
import jax
import jax.numpy as jnp
from jax import lax
from jax.sharding import PartitionSpec as P


def with_halo(cells, sides, width):
    for axis, dim in sides:
        count = lax.axis_size(axis)
        ends = count - 1
        head = lax.slice_in_dim(cells, 0, width, axis=dim)
        tail = lax.slice_in_dim(cells, cells.shape[dim] - width, cells.shape[dim], axis=dim)
        cells = jnp.concatenate(
            [
                lax.ppermute(tail, axis, [(i, (i + 1) % count) for i in range(ends)]),
                cells,
                lax.ppermute(head, axis, [((i + 1) % count, i) for i in range(ends)]),
            ],
            axis=dim,
        )
    return cells


def extend_tile(source, spread):
    return with_halo(source, (("row", 0), ("col", 1)), spread)


def mirror_tile(summed):
    extent = summed.shape[0]
    channels = summed.shape[2]
    pieces = lax.axis_size("row")
    stacked = summed.reshape(pieces, 1, extent // pieces, extent, channels)
    moved = lax.all_to_all(
        lax.all_to_all(stacked, "row", split_axis=0, concat_axis=1, tiled=True),
        "col",
        split_axis=1,
        concat_axis=0,
        tiled=True,
    )
    arrived = lax.all_to_all(moved, "row", split_axis=0, concat_axis=1, tiled=True)
    return jnp.swapaxes(arrived.reshape(extent, extent, channels), 0, 1)


def residual_sum(extended, source, kernel, conv_bias, mixer, mix_bias, spread):
    extent = source.shape[0]
    channels = source.shape[2]
    total = jnp.zeros((extent * extent, channels), jnp.float32)
    for tap_row in range(3):
        for tap_col in range(3):
            window = extended[
                tap_row * spread : tap_row * spread + extent,
                tap_col * spread : tap_col * spread + extent,
                :,
            ]
            total = total + jnp.dot(
                window.reshape(extent * extent, channels),
                kernel[tap_row, tap_col],
                preferred_element_type=jnp.float32,
            )
    activated = jax.nn.relu(total + conv_bias).astype(jnp.bfloat16)
    mixed = jnp.dot(activated, mixer, preferred_element_type=jnp.float32) + mix_bias
    summed = (source.reshape(extent * extent, channels).astype(jnp.float32) + mixed).astype(
        jnp.bfloat16
    )
    return summed.reshape(extent, extent, channels)


def run_block(source, kernel, conv_bias, mixer, mix_bias, spread, symmetric):
    extended = extend_tile(source, spread)
    summed = residual_sum(extended, source, kernel, conv_bias, mixer, mix_bias, spread)
    if symmetric:
        other = residual_sum(
            jnp.swapaxes(extended, 0, 1),
            jnp.swapaxes(source, 0, 1),
            kernel,
            conv_bias,
            mixer,
            mix_bias,
            spread,
        )
        mirrored = jnp.swapaxes(other, 0, 1)
    else:
        mirrored = mirror_tile(summed)
    return jax.nn.relu((summed.astype(jnp.float32) + mirrored.astype(jnp.float32)) * 0.5)


def body(
    features,
    kernel_first,
    bias_first,
    mixer_first,
    shift_first,
    kernel_second,
    bias_second,
    mixer_second,
    shift_second,
):
    first = run_block(
        features, kernel_first, bias_first, mixer_first, shift_first, 2, False
    ).astype(jnp.bfloat16)
    return run_block(first, kernel_second, bias_second, mixer_second, shift_second, 4, True)


def solution(mesh):
    return jax.shard_map(
        body,
        mesh=mesh,
        in_specs=(P(("groups", "row"), "col", None), P(), P(), P(), P(), P(), P(), P(), P()),
        out_specs=P(("groups", "row"), "col", None),
        check_vma=False,
    )
```

profile of v0, /device:TPU:17, one launch (start us, length us, event | category | flops | bytes accessed | tf_op | source)
XLA Modules:
  0.0 154.4 jit_solution(14405824788707856362)
XLA Ops:
  0.0 0.8 fusion.108
  0.8 3.7 %collective-permute-start = (bf16[2,64,128]{2,1,0:T(8,128)(2,1)S(1)}, bf16[2,64,128]{2,1,0:T(8,128)(2,1)S(1)}, u32[]{:S(2)}, u32[]{:S(2)}) collective-permute-start(bf16[2,64,128]{2,1,0:T(8,128)(2,1)S(1)} %get-tuple-element.45), channel_id=1, source_target_pairs={{0,4},{4,8},{8,12},{1,5},{5,9},{9,13},{2,6},{6,10},{10,14},{3,7},{... | collective-permute-start | bytes 98312 | tf_op jit(solution)/shard_map/ppermute | solution.py:15
  4.5 1.9 %collective-permute-start.1 = (bf16[2,64,128]{2,1,0:T(8,128)(2,1)S(1)}, bf16[2,64,128]{2,1,0:T(8,128)(2,1)S(1)}, u32[]{:S(2)}, u32[]{:S(2)}) collective-permute-start(bf16[2,64,128]{2,1,0:T(8,128)(2,1)S(1)} %get-tuple-element.44), channel_id=1, source_target_pairs={{4,0},{8,4},{12,8},{5,1},{9,5},{13,9},{6,2},{10,6},{14,10},{7,3},{... | collective-permute-start | bytes 98312 | tf_op jit(solution)/shard_map/ppermute | solution.py:17
  6.4 3.3 %collective-permute-done.1 = bf16[2,64,128]{2,1,0:T(8,128)(2,1)S(1)} collective-permute-done((bf16[2,64,128]{2,1,0:T(8,128)(2,1)S(1)}, bf16[2,64,128]{2,1,0:T(8,128)(2,1)S(1)}, u32[]{:S(2)}, u32[]{:S(2)}) %collective-permute-start.1) | collective-permute-done | bytes 32800 | tf_op jit(solution)/shard_map/ppermute | solution.py:17
  9.7 3.1 %pad_maximum_fusion.6 = (bf16[64,64,128]{2,1,0:T(8,128)(2,1)S(1)}, bf16[68,64,128]{2,1,0:T(8,128)(2,1)S(1)}, bf16[64,64,128]{2,1,0:T(8,128)(2,1)S(1)}) fusion(bf16[64,64,128]{2,1,0:T(8,128)(2,1)} %param.9, bf16[2,64,128]{2,1,0:T(8,128)(2,1)S(1)} %collective-permute-done, bf16[68,64,128]{2,1,0:T(8,128)(2,1)S(1)} %constant_dynamic-update-slice_fusion.2, ...), kind=kLoop, calls=%fused_computation.70 | loop fusion | flops 4194304 | bytes 4259840 | tf_op jit(solution)/shard_map/concatenate | solution.py:13
  12.9 3.2 %collective-permute-start.2 = (bf16[68,2,128]{2,1,0:T(2,128)(2,1)S(1)}, bf16[68,2,128]{2,1,0:T(2,128)(2,1)S(1)}, u32[]{:S(2)}, u32[]{:S(2)}) collective-permute-start(bf16[68,2,128]{2,1,0:T(2,128)(2,1)S(1)} %get-tuple-element.35), channel_id=1, source_target_pairs={{0,1},{1,2},{2,3},{4,5},{5,6},{6,7},{8,9},{9,10},{10,11},{12,13},{... | collective-permute-start | bytes 104456 | tf_op jit(solution)/shard_map/ppermute | solution.py:15
  16.1 2.1 %collective-permute-start.3 = (bf16[68,2,128]{2,1,0:T(2,128)(2,1)S(1)}, bf16[68,2,128]{2,1,0:T(2,128)(2,1)S(1)}, u32[]{:S(2)}, u32[]{:S(2)}) collective-permute-start(bf16[68,2,128]{2,1,0:T(2,128)(2,1)S(1)} %get-tuple-element.36), channel_id=1, source_target_pairs={{1,0},{2,1},{3,2},{5,4},{6,5},{7,6},{9,8},{10,9},{11,10},{13,12},{... | collective-permute-start | bytes 104456 | tf_op jit(solution)/shard_map/ppermute | solution.py:17
  18.2 1.8 %fusion.58 = f32[4096,128]{1,0:T(8,128)} fusion(bf16[4096,128]{1,0:T(8,128)(2,1)S(1)} %bitcast.188, bf16[3,3,128,128]{3,2,1,0:T(8,128)(2,1)S(1)} %copy-done.9), kind=kOutput, calls=%fused_computation.103 | convolution fusion | flops 134217728 | bytes 3178496 | tf_op jit(solution)/shard_map/dot_general | solution.py:55
  20.8 3.2 %pad_maximum_fusion.5 = (bf16[64,64,128]{2,1,0:T(8,128)(2,1)S(1)}, bf16[64,64,128]{2,1,0:T(8,128)(2,1)S(1)}, bf16[64,64,128]{2,1,0:T(8,128)(2,1)S(1)}, bf16[64,6...) fusion(bf16[68,64,128]{2,1,0:T(8,128)(2,1)S(1)} %constant_dynamic-update-slice_fusion,, ...), kind=kLoop, calls=%fused_computation.69 | loop fusion | flops 12582912 | bytes 7475200 | tf_op jit(solution)/shard_map/concatenate | solution.py:13
  24.0 1.7 %fusion.56 = f32[4096,128]{1,0:T(8,128)} fusion(bf16[4096,128]{1,0:T(8,128)(2,1)S(1)} %bitcast.175, bf16[3,3,128,128]{3,2,1,0:T(8,128)(2,1)S(1)} %copy-done.9), kind=kOutput, calls=%fused_computation.101 | convolution fusion | flops 134217728 | bytes 3178496 | tf_op jit(solution)/shard_map/dot_general | solution.py:55
  27.0 0.8 copy-done.1
  28.2 1.7 %convolution_add_fusion.19 = f32[4096,128]{1,0:T(8,128)} fusion(f32[4096,128]{1,0:T(8,128)S(1)} %convolution_add_fusion.20, bf16[4096,128]{1,0:T(8,128)(2,1)S(1)} %bitcast.171, bf16[3,3,128,128]{3,2,1,0:T(8,128)(2,1)S(1)} %copy-done.9), kind=kOutput, calls=%fused_computation.31 | convolution fusion | flops 134742016 | bytes 5275648 | tf_op jit(solution)/shard_map/dot_general | solution.py:55
  30.0 3.7 %fusion.13 = bf16[4096,128]{1,0:T(8,128)(2,1)S(1)} fusion(bf16[128,128]{1,0:T(8,128)(2,1)S(1)} %copy-done.10, bf16[4096,128]{1,0:T(8,128)(2,1)S(1)} %bitcast.160, f32[4096,128]{1,0:T(8,128)} %fusion.56, f32[4096,128]{1,0:T(8,128)} %fusion.58, f32[4096,128]{1,0:T(8,128)} %convolution_add_fusion.19, bf16[4096,128]{1,0:T(8,128)(2,1)S(1)} %bitcast.170, ...), kind=kOutput, calls=%fused_computation.37 | convolution fusion | flops 273678336 | bytes 9503744 | tf_op jit(solution)/shard_map/dot_general | solution.py:61
  33.7 16.3 %all_to_all.33 = bf16[4,1,16,64,128]{4,3,2,1,0:T(8,128)(2,1)S(1)} all-to-all(bf16[4,1,16,64,128]{4,3,2,1,0:T(8,128)(2,1)S(1)} %bitcast.161), channel_id=1, replica_groups=mesh['groups'=2,'row'=4,'col'=4] {'row'}, dimensions={0} | all-to-all | bytes 2097152 | tf_op jit(solution)/shard_map/all_to_all | solution.py:34
  50.0 26.2 %all_to_all.34 = bf16[1,4,16,64,128]{4,3,2,0,1:T(8,128)(2,1)S(1)} all-to-all(bf16[1,4,16,64,128]{4,3,2,0,1:T(8,128)(2,1)S(1)} %bitcast.192), channel_id=1, replica_groups=mesh['groups'=2,'row'=4,'col'=4] {'col'}, dimensions={1} | all-to-all | bytes 2097152 | tf_op jit(solution)/shard_map/all_to_all | solution.py:33
  76.2 17.3 %all_to_all.35 = bf16[4,1,16,64,128]{4,3,2,1,0:T(8,128)(2,1)S(1)} all-to-all(bf16[4,1,16,64,128]{4,3,2,1,0:T(8,128)(2,1)S(1)} %bitcast.191), channel_id=1, replica_groups=mesh['groups'=2,'row'=4,'col'=4] {'row'}, dimensions={0} | all-to-all | bytes 2097152 | tf_op jit(solution)/shard_map/all_to_all | solution.py:40
  94.7 2.9 %collective-permute-start.5 = (bf16[4,64,128]{2,1,0:T(8,128)(2,1)S(1)}, bf16[4,64,128]{2,1,0:T(8,128)(2,1)S(1)}, u32[]{:S(2)}, u32[]{:S(2)}) collective-permute-start(bf16[4,64,128]{2,1,0:T(8,128)(2,1)S(1)} %get-tuple-element.40), channel_id=1, source_target_pairs={{4,0},{8,4},{12,8},{5,1},{9,5},{13,9},{6,2},{10,6},{14,10},{7,3},{... | collective-permute-start | bytes 196616 | tf_op jit(solution)/shard_map/ppermute | solution.py:17
  97.7 2.6 %collective-permute-start.4 = (bf16[4,64,128]{2,1,0:T(8,128)(2,1)S(1)}, bf16[4,64,128]{2,1,0:T(8,128)(2,1)S(1)}, u32[]{:S(2)}, u32[]{:S(2)}) collective-permute-start(bf16[4,64,128]{2,1,0:T(8,128)(2,1)S(1)} %get-tuple-element.39), channel_id=1, source_target_pairs={{0,4},{4,8},{8,12},{1,5},{5,9},{9,13},{2,6},{6,10},{10,14},{3,7},{... | collective-permute-start | bytes 196616 | tf_op jit(solution)/shard_map/ppermute | solution.py:15
  100.3 1.2 copy.33
  101.7 3.4 %collective-permute-start.6 = (bf16[72,4,128]{2,1,0:T(4,128)(2,1)S(1)}, bf16[72,4,128]{2,1,0:T(4,128)(2,1)S(1)}, u32[]{:S(2)}, u32[]{:S(2)}) collective-permute-start(bf16[72,4,128]{2,1,0:T(4,128)(2,1)S(1)} %get-tuple-element.24), channel_id=1, source_target_pairs={{0,1},{1,2},{2,3},{4,5},{5,6},{6,7},{8,9},{9,10},{10,11},{12,13},{... | collective-permute-start | bytes 221192 | tf_op jit(solution)/shard_map/ppermute | solution.py:15
  105.2 2.1 %collective-permute-start.7 = (bf16[72,4,128]{2,1,0:T(4,128)(2,1)S(1)}, bf16[72,4,128]{2,1,0:T(4,128)(2,1)S(1)}, u32[]{:S(2)}, u32[]{:S(2)}) collective-permute-start(bf16[72,4,128]{2,1,0:T(4,128)(2,1)S(1)} %get-tuple-element.25), channel_id=1, source_target_pairs={{1,0},{2,1},{3,2},{5,4},{6,5},{7,6},{9,8},{10,9},{11,10},{13,12},{... | collective-permute-start | bytes 221192 | tf_op jit(solution)/shard_map/ppermute | solution.py:17
  107.3 1.2 pad_maximum_fusion.1
  108.4 1.8 %fusion.51 = f32[4096,128]{1,0:T(8,128)} fusion(bf16[4096,128]{1,0:T(8,128)(2,1)S(1)} %bitcast.177, bf16[3,3,128,128]{3,2,1,0:T(8,128)(2,1)S(1)} %copy-done.8), kind=kOutput, calls=%fused_computation.96 | convolution fusion | flops 134217728 | bytes 3178496 | tf_op jit(solution)/shard_map/dot_general | solution.py:55
  110.2 0.7 collective-permute-done.7
  110.9 2.0 %maximum_maximum_fusion = (bf16[72,68,128]{2,1,0:T(8,128)(2,1)S(1)}, bf16[72,68,128]{2,1,0:T(8,128)(2,1)S(1)}) fusion(bf16[4,64,128]{2,1,0:T(8,128)(2,1)S(1)} %collective-permute-done.5, bf16[64,64,128]{2,1,0:T(8,128)(2,1)S(1)} %get-tuple-element.6, bf16[4,64,128]{2,1,0:T(8,128)(2,1)S(1)} %collective-permute-done.4, ...), kind=kLoop, calls=%fused_computation.54 | loop fusion | flops 10027008 | bytes 3833856 | tf_op jit(solution)/shard_map/concatenate | solution.py:13
  112.9 3.1 %fusion.104 = (bf16[64,64,128]{2,1,0:T(8,128)(2,1)}, bf16[64,64,128]{2,1,0:T(8,128)(2,1)}, bf16[64,64,128]{2,1,0:T(8,128)(2,1)}, bf16[64,64,128]{2,1,0:T(8,128)(...) fusion(bf16[72,68,128]{2,1,0:T(8,128)(2,1)S(1)} %get-tuple-element.22, ...), kind=kLoop, calls=%fused_computation.147 | loop fusion | bytes 12582912 | tf_op jit(solution)/shard_map/slice | solution.py:50
  116.0 1.7 %fusion.35 = f32[4096,128]{1,0:T(8,128)} fusion(bf16[4096,128]{1,0:T(8,128)(2,1)S(1)} %bitcast.176, bf16[3,3,128,128]{3,2,1,0:T(8,128)(2,1)S(1)} %copy-done.8), kind=kOutput, calls=%fused_computation.81 | convolution fusion | flops 134217728 | bytes 3178496 | tf_op jit(solution)/shard_map/dot_general | solution.py:55
  117.7 0.7 maximum_bitcast_fusion
  118.4 2.8 %fusion.103 = (bf16[64,64,128]{2,0,1:T(8,128)(2,1)S(1)}, bf16[64,64,128]{2,0,1:T(8,128)(2,1)S(1)}, bf16[64,64,128]{2,0,1:T(8,128)(2,1)S(1)}, bf16[64,64,128]{2,0...) fusion(bf16[72,72,128]{2,0,1:T(8,128)(2,1)S(1)} %maximum_bitcas, ...), kind=kLoop, calls=%fused_computation.146 | loop fusion | bytes 18874368 | tf_op jit(solution)/shard_map/slice | solution.py:50
  121.2 0.7 copy.34
  122.3 0.7 copy.35
  123.0 0.7 copy.36
  123.7 0.7 copy.37
  124.4 0.7 copy.38
  125.1 0.7 copy.39
  125.7 0.7 copy.40
  126.4 0.7 copy.41
  127.1 1.7 %copy.42 = bf16[64,64,128]{2,1,0:T(8,128)(2,1)} copy(bf16[64,64,128]{2,0,1:T(8,128)(2,1)S(1)} %get-tuple-element.7) | data formatting | bytes 2097152 | tf_op jit(solution)/shard_map/slice | solution.py:50
  131.3 1.7 %convolution_add_fusion.2 = f32[4096,128]{1,0:T(8,128)} fusion(f32[4096,128]{1,0:T(8,128)S(1)} %convolution_add_fusion.3, bf16[4096,128]{1,0:T(8,128)(2,1)S(1)} %bitcast.178, bf16[3,3,128,128]{3,2,1,0:T(8,128)(2,1)S(1)} %copy-done.8), kind=kOutput, calls=%fused_computation.5 | convolution fusion | flops 134742016 | bytes 5275648 | tf_op jit(solution)/shard_map/dot_general | solution.py:55
  133.1 3.7 %fusion.17 = bf16[4096,128]{1,0:T(8,128)(2,1)} fusion(f32[4096,128]{1,0:T(8,128)S(1)} %bitcast.164, bf16[128,128]{1,0:T(8,128)(2,1)S(1)} %copy-done, f32[4096,128]{1,0:T(8,128)} %convolution_add_fusion.2, bf16[4096,128]{1,0:T(8,128)(2,1)} %bitcast.193, f32[128]{0:T(128)S(1)} %copy-done.11, f32[128]{0:T(128)S(1)} %copy-done.12, ...), kind=kOutput, calls=%fused_computation.41 | convolution fusion | flops 272105472 | bytes 6358016 | tf_op jit(solution)/shard_map/dot_general | solution.py:61
  136.8 1.6 %convert.10 = f32[64,64,128]{2,1,0:T(8,128)S(1)} convert(bf16[64,64,128]{2,1,0:T(8,128)(2,1)} %bitcast.190) | non-fusion elementwise | flops 524288 | bytes 3145728 | tf_op jit(solution)/shard_map/convert_element_type | solution.py:84
  139.4 0.8 copy-done.6
  140.6 0.8 copy-done.5
  142.3 0.8 copy-done.4
  143.5 0.8 copy-done.3
  144.3 1.8 %convolution_add_fusion.11 = f32[4096,128]{1,0:T(8,128)} fusion(f32[4096,128]{1,0:T(8,128)S(1)} %convolution_add_fusion.12, bf16[4096,128]{1,0:T(8,128)(2,1)S(1)} %bitcast.165, bf16[3,3,128,128]{3,2,1,0:T(8,128)(2,1)S(1)} %copy-done.8), kind=kOutput, calls=%fused_computation.18 | convolution fusion | flops 134742016 | bytes 5275648 | tf_op jit(solution)/shard_map/dot_general | solution.py:55
  146.1 4.4 %fusion.15 = bf16[4096,128]{1,0:T(8,128)(2,1)} fusion(bf16[128,128]{1,0:T(8,128)(2,1)S(1)} %copy-done, bf16[4096,128]{1,0:T(8,128)(2,1)S(1)} %bitcast.158, f32[4096,128]{1,0:T(8,128)} %fusion.35, f32[4096,128]{1,0:T(8,128)} %convolution_add_fusion.11, bf16[4096,128]{1,0:T(8,128)(2,1)} %bitcast.186, f32[128]{0:T(128)S(1)} %copy-done.11, ...), kind=kOutput, calls=%fused_computation.39 | convolution fusion | flops 273154048 | bytes 7406592 | tf_op jit(solution)/shard_map/dot_general | solution.py:61
  150.4 4.0 %fusion.19 = f32[64,64,128]{2,1,0:T(8,128)} fusion(bf16[64,64,128]{2,1,0:T(8,128)(2,1)} %bitcast.189, f32[64,64,128]{2,1,0:T(8,128)S(1)} %convert.10), kind=kLoop, calls=%fused_computation.44 | loop fusion | flops 2097152 | bytes 5242880 | tf_op jit(solution)/shard_map/jit(relu)/max | solution.py:84
  (55 shorter events, 9.4 us)
Async XLA Ops:
  0.0 133.1 %copy-start = (bf16[128,128]{1,0:T(8,128)(2,1)S(1)}, bf16[128,128]{1,0:T(8,128)(2,1)}, u32[]{:S(2)}) copy-start(bf16[128,128]{1,0:T(8,128)(2,1)} %param.16) | copy-start | bytes 98308
  0.8 5.6 %collective-permute-start = (bf16[2,64,128]{2,1,0:T(8,128)(2,1)S(1)}, bf16[2,64,128]{2,1,0:T(8,128)(2,1)S(1)}, u32[]{:S(2)}, u32[]{:S(2)}) collective-permute-start(bf16[2,64,128]{2,1,0:T(8,128)(2,1)S(1)} %get-tuple-element.45), channel_id=1, source_target_pairs={{0,4},{4,8},{8,12},{1,5},{5,9},{9,13},{2,6},{6,10},{10,14},{3,7},{... | collective-permute-start | bytes 98312 | tf_op jit(solution)/shard_map/ppermute | solution.py:15
  4.5 5.2 %collective-permute-start.1 = (bf16[2,64,128]{2,1,0:T(8,128)(2,1)S(1)}, bf16[2,64,128]{2,1,0:T(8,128)(2,1)S(1)}, u32[]{:S(2)}, u32[]{:S(2)}) collective-permute-start(bf16[2,64,128]{2,1,0:T(8,128)(2,1)S(1)} %get-tuple-element.44), channel_id=1, source_target_pairs={{4,0},{8,4},{12,8},{5,1},{9,5},{13,9},{6,2},{10,6},{14,10},{7,3},{... | collective-permute-start | bytes 98312 | tf_op jit(solution)/shard_map/ppermute | solution.py:17
  6.4 11.8 %copy-start.9 = (bf16[3,3,128,128]{3,2,1,0:T(8,128)(2,1)S(1)}, bf16[3,3,128,128]{3,2,1,0:T(8,128)(2,1)}, u32[]{:S(2)}) copy-start(bf16[3,3,128,128]{3,2,1,0:T(8,128)(2,1)} %param.10) | copy-start | bytes 884740
  12.9 7.5 %collective-permute-start.2 = (bf16[68,2,128]{2,1,0:T(2,128)(2,1)S(1)}, bf16[68,2,128]{2,1,0:T(2,128)(2,1)S(1)}, u32[]{:S(2)}, u32[]{:S(2)}) collective-permute-start(bf16[68,2,128]{2,1,0:T(2,128)(2,1)S(1)} %get-tuple-element.35), channel_id=1, source_target_pairs={{0,1},{1,2},{2,3},{4,5},{5,6},{6,7},{8,9},{9,10},{10,11},{12,13},{... | collective-permute-start | bytes 104456 | tf_op jit(solution)/shard_map/ppermute | solution.py:15
  16.1 4.7 %collective-permute-start.3 = (bf16[68,2,128]{2,1,0:T(2,128)(2,1)S(1)}, bf16[68,2,128]{2,1,0:T(2,128)(2,1)S(1)}, u32[]{:S(2)}, u32[]{:S(2)}) collective-permute-start(bf16[68,2,128]{2,1,0:T(2,128)(2,1)S(1)} %get-tuple-element.36), channel_id=1, source_target_pairs={{1,0},{2,1},{3,2},{5,4},{6,5},{7,6},{9,8},{10,9},{11,10},{13,12},{... | collective-permute-start | bytes 104456 | tf_op jit(solution)/shard_map/ppermute | solution.py:17
  26.5 1.2 copy-start.1
  28.2 1.8 %copy-start.10 = (bf16[128,128]{1,0:T(8,128)(2,1)S(1)}, bf16[128,128]{1,0:T(8,128)(2,1)}, u32[]{:S(2)}) copy-start(bf16[128,128]{1,0:T(8,128)(2,1)} %param.12) | copy-start | bytes 98308
  28.2 1.8 %copy-start.13 = (f32[128]{0:T(128)S(1)}, f32[128]{0:T(128)}, u32[]{:S(2)}) copy-start(f32[128]{0:T(128)} %param.13) | copy-start | bytes 1540
  28.2 1.8 %copy-start.14 = (f32[128]{0:T(128)S(1)}, f32[128]{0:T(128)}, u32[]{:S(2)}) copy-start(f32[128]{0:T(128)} %param.11) | copy-start | bytes 1540
  94.7 6.8 %collective-permute-start.5 = (bf16[4,64,128]{2,1,0:T(8,128)(2,1)S(1)}, bf16[4,64,128]{2,1,0:T(8,128)(2,1)S(1)}, u32[]{:S(2)}, u32[]{:S(2)}) collective-permute-start(bf16[4,64,128]{2,1,0:T(8,128)(2,1)S(1)} %get-tuple-element.40), channel_id=1, source_target_pairs={{4,0},{8,4},{12,8},{5,1},{9,5},{13,9},{6,2},{10,6},{14,10},{7,3},{... | collective-permute-start | bytes 196616 | tf_op jit(solution)/shard_map/ppermute | solution.py:17
  97.7 3.9 %collective-permute-start.4 = (bf16[4,64,128]{2,1,0:T(8,128)(2,1)S(1)}, bf16[4,64,128]{2,1,0:T(8,128)(2,1)S(1)}, u32[]{:S(2)}, u32[]{:S(2)}) collective-permute-start(bf16[4,64,128]{2,1,0:T(8,128)(2,1)S(1)} %get-tuple-element.39), channel_id=1, source_target_pairs={{0,4},{4,8},{8,12},{1,5},{5,9},{9,13},{2,6},{6,10},{10,14},{3,7},{... | collective-permute-start | bytes 196616 | tf_op jit(solution)/shard_map/ppermute | solution.py:15
  101.6 6.9 %copy-start.8 = (bf16[3,3,128,128]{3,2,1,0:T(8,128)(2,1)S(1)}, bf16[3,3,128,128]{3,2,1,0:T(8,128)(2,1)}, u32[]{:S(2)}) copy-start(bf16[3,3,128,128]{3,2,1,0:T(8,128)(2,1)} %param.14) | copy-start | bytes 884740
  101.7 8.5 %collective-permute-start.6 = (bf16[72,4,128]{2,1,0:T(4,128)(2,1)S(1)}, bf16[72,4,128]{2,1,0:T(4,128)(2,1)S(1)}, u32[]{:S(2)}, u32[]{:S(2)}) collective-permute-start(bf16[72,4,128]{2,1,0:T(4,128)(2,1)S(1)} %get-tuple-element.24), channel_id=1, source_target_pairs={{0,1},{1,2},{2,3},{4,5},{5,6},{6,7},{8,9},{9,10},{10,11},{12,13},{... | collective-permute-start | bytes 221192 | tf_op jit(solution)/shard_map/ppermute | solution.py:15
  105.2 5.8 %collective-permute-start.7 = (bf16[72,4,128]{2,1,0:T(4,128)(2,1)S(1)}, bf16[72,4,128]{2,1,0:T(4,128)(2,1)S(1)}, u32[]{:S(2)}, u32[]{:S(2)}) collective-permute-start(bf16[72,4,128]{2,1,0:T(4,128)(2,1)S(1)} %get-tuple-element.25), channel_id=1, source_target_pairs={{1,0},{2,1},{3,2},{5,4},{6,5},{7,6},{9,8},{10,9},{11,10},{13,12},{... | collective-permute-start | bytes 221192 | tf_op jit(solution)/shard_map/ppermute | solution.py:17
  131.3 1.8 %copy-start.11 = (f32[128]{0:T(128)S(1)}, f32[128]{0:T(128)}, u32[]{:S(2)}) copy-start(f32[128]{0:T(128)} %param.17) | copy-start | bytes 1540
  131.3 1.8 %copy-start.12 = (f32[128]{0:T(128)S(1)}, f32[128]{0:T(128)}, u32[]{:S(2)}) copy-start(f32[128]{0:T(128)} %param.15) | copy-start | bytes 1540
  136.8 1.9 %copy-start.2 = (f32[4096,128]{1,0:T(8,128)S(1)}, f32[4096,128]{1,0:T(8,128)}, u32[]{:S(2)}) copy-start(f32[4096,128]{1,0:T(8,128)} %fusion.51) | copy-start | bytes 6291460
  136.8 2.2 %copy-start.7 = (bf16[64,64,128]{2,1,0:T(8,128)(2,1)S(1)}, bf16[64,64,128]{2,1,0:T(8,128)(2,1)}, u32[]{:S(2)}) copy-start(bf16[64,64,128]{2,1,0:T(8,128)(2,1)} %get-tuple-element.18) | copy-start | bytes 3145732
  139.0 1.2 copy-start.6
  140.2 1.2 copy-start.5
  141.8 1.2 copy-start.4
  143.1 1.2 copy-start.3
where the time goes:
time: 158 us; the launch traced here: 154 us
  blocking collectives  59.8 us (38%)
  matrix products  31.1 us (20%)
  starting transfers between devices  22 us (14%)
  local copies, waits for them, and re-layouts  20.2 us (13%)
  other arithmetic  16.4 us (10%)
  waiting for transfers between devices  4.42 us (3%)
    all_to_all x1, blocking collectives, mirror_tile(): lax.all_to_all(lax.all_to_all(stacked, 'row', split_axis=0, concat_axis=1...  26.2 us
    dot_general x24, matrix products, residual_sum(): jnp.dot(window.reshape(extent * extent, channels), kernel[tap_row, tap_co...  19.3 us
    all_to_all x1, blocking collectives, mirror_tile(): lax.all_to_all(moved, 'row', split_axis=0, concat_axis=1, tiled=True)  17.3 us
    all_to_all x1, blocking collectives, mirror_tile(): lax.all_to_all(stacked, 'row', split_axis=0, concat_axis=1, tiled=True)  16.3 us
    slice x11, local copies, waits for them, and re-layouts, residual_sum(): extended[tap_row * spread:tap_row * spread + extent, tap_col * spread:tap...  12.9 us
    ppermute x4, starting transfers between devices, with_halo(): lax.ppermute(tail, axis, [(i, (i + 1) % count) for i in range(ends)])  12.9 us
    dot_general x3, matrix products, residual_sum(): jnp.dot(activated, mixer, preferred_element_type=jnp.float32) + mix_bias  11.8 us
    concatenate x4, other arithmetic, with_halo(): jnp.concatenate([lax.ppermute(tail, axis, [(i, (i + 1) % count) for i in...  9.44 us
  transfers between devices with their start and end apart: 8, of which 4 were waited for; matrix products, arithmetic and copies ran while one was open for 4% of the time, Pallas kernels for 0%

commit v1 on v0

v1 whole, which is shorter than its diff:
```python
import functools

import jax
import jax.numpy as jnp
from jax import lax
from jax.experimental import pallas as pl
from jax.experimental.pallas import tpu as pltpu
from jax.sharding import PartitionSpec as P

MESH = pl.DeviceIdType.MESH
FIRST, SECOND = 2, 4
BLOCK = 16


def pack(edge, at, width):
    per = 8 // width
    rows, _, channels = edge.shape
    parts = edge.reshape(rows // per, per, 8, channels)
    lane = lax.broadcasted_iota(jnp.int32, (rows // per, 8, channels), 1)
    packed = None
    for m in range(per):
        shift = (m * width - at) % 8
        part = parts[:, m]
        part = pltpu.roll(part, shift, 1) if shift else part
        packed = part if m == 0 else jnp.where(lane >= m * width, part, packed)
    return packed.reshape(rows * width, channels).astype(jnp.bfloat16)


def unpack(packed, at, width):
    per = 8 // width
    tiles = packed.shape[0] // 8
    channels = packed.shape[1]
    packed = packed.astype(jnp.float32).reshape(tiles, 8, channels)
    parts = []
    for m in range(per):
        shift = (at - m * width) % 8
        parts.append(pltpu.roll(packed, shift, 1) if shift else packed)
    return jnp.stack(parts, axis=1).reshape(tiles * per, 8, channels)


def patch(shifted, spread, lo, rows, left, right):
    extent = shifted.shape[2]
    channels = shifted.shape[3]
    lane = lax.broadcasted_iota(jnp.int32, (rows, 16, channels), 1)
    at = pl.ds(spread + lo, rows)
    strip = unpack(left, 0, spread)
    old = shifted[0, at, 0:16, :].astype(jnp.float32)
    new = jnp.where(lane < spread, jnp.concatenate([strip, strip], axis=1), old)
    shifted[0, at, 0:16, :] = new.astype(jnp.bfloat16)
    strip = unpack(right, 8 - spread, spread)
    old = shifted[2, at, extent - 16 : extent, :].astype(jnp.float32)
    new = jnp.where(lane >= 16 - spread, jnp.concatenate([strip, strip], axis=1), old)
    shifted[2, at, extent - 16 : extent, :] = new.astype(jnp.bfloat16)


def kernel(
    x, k1, b1, m1, s1, k2, b2, m2, s2, out,
    xs1, xs2, h, mir, flip, w2, so1, si1, so2, si2,
    strip_send, strip_recv, rows_send, rows_recv, mir_send, mir_recv,
):
    extent, _, channels = x.shape
    chunks = extent // BLOCK
    order = [0] + [chunks - 1] * (chunks > 1) + list(range(1, chunks - 1))
    r, c = lax.axis_index("row"), lax.axis_index("col")
    nr, nc = lax.axis_size("row"), lax.axis_size("col")
    has_up, has_down, has_left, has_right = r > 0, r < nr - 1, c > 0, c < nc - 1
    up, down = {"row": r - 1}, {"row": r + 1}
    left, right = {"col": c - 1}, {"col": c + 1}
    mirror = {"row": c, "col": r}
    off = r != c

    barrier = pltpu.get_barrier_semaphore()
    peers = ((has_up, up), (has_down, down), (has_left, left), (has_right, right), (off, mirror))
    for has, peer in peers:
        @pl.when(has)
        def _():
            pl.semaphore_signal(barrier, inc=1, device_id=peer, device_id_type=MESH)
    count = sum(has.astype(jnp.int32) for has, _ in peers)

    so1[0] = pack(x[:, 0:16, :].astype(jnp.float32)[:, 0:8], 0, FIRST)
    so1[1] = pack(x[:, extent - 16 : extent, :].astype(jnp.float32)[:, 8:16], 8 - FIRST, FIRST)
    pl.semaphore_wait(barrier, count)

    def strips(src, dst, n):
        return (
            (has_left, pltpu.make_async_remote_copy(
                src.at[0], dst.at[1], strip_send.at[n, 0], strip_recv.at[n, 1],
                device_id=left, device_id_type=MESH)),
            (has_right, pltpu.make_async_remote_copy(
                src.at[1], dst.at[0], strip_send.at[n, 1], strip_recv.at[n, 0],
                device_id=right, device_id_type=MESH)),
        )

    def start(copies):
        for has, copy in copies:
            @pl.when(has)
            def _():
                copy.start()

    def finish_strips(copies, dst):
        (hl, to_left), (hr, to_right) = copies

        @pl.when(hl)
        def _():
            to_left.wait_send()
            to_right.wait_recv()

        @pl.when(hr)
        def _():
            to_right.wait_send()
            to_left.wait_recv()

        @pl.when(jnp.logical_not(hl))
        def _():
            dst[0] = jnp.zeros(dst.shape[1:], dst.dtype)

        @pl.when(jnp.logical_not(hr))
        def _():
            dst[1] = jnp.zeros(dst.shape[1:], dst.dtype)

    def halo_rows(shifted, spread, n):
        return (
            (has_up, pltpu.make_async_remote_copy(
                shifted.at[:, spread : 2 * spread], shifted.at[:, extent + spread : extent + 2 * spread],
                rows_send.at[n, 0], rows_recv.at[n, 1], device_id=up, device_id_type=MESH)),
            (has_down, pltpu.make_async_remote_copy(
                shifted.at[:, extent : extent + spread], shifted.at[:, 0:spread],
                rows_send.at[n, 1], rows_recv.at[n, 0], device_id=down, device_id_type=MESH)),
        )

    def finish_rows(copies, shifted, spread):
        (hu, to_up), (hd, to_down) = copies
        zeros = jnp.zeros((3, spread) + shifted.shape[2:], shifted.dtype)

        @pl.when(hu)
        def _():
            to_up.wait_send()
            to_down.wait_recv()

        @pl.when(hd)
        def _():
            to_down.wait_send()
            to_up.wait_recv()

        @pl.when(jnp.logical_not(hu))
        def _():
            shifted[:, 0:spread] = zeros

        @pl.when(jnp.logical_not(hd))
        def _():
            shifted[:, extent + spread : extent + 2 * spread] = zeros

    def spread_rows(shifted, spread, at, cells):
        shifted[1, at] = cells.astype(jnp.bfloat16)
        shifted[0, at] = pltpu.roll(cells, spread, 1).astype(jnp.bfloat16)
        shifted[2, at] = pltpu.roll(cells, extent - spread, 1).astype(jnp.bfloat16)

    first_strips = strips(so1, si1, 0)
    start(first_strips)

    @pl.loop(0, extent // 4)
    def _(step):
        spread_rows(xs1, FIRST, pl.ds(FIRST + step * 4, 4), x[pl.ds(step * 4, 4)].astype(jnp.float32))

    finish_strips(first_strips, si1)

    for k in range(chunks):
        n = BLOCK * FIRST
        patch(xs1, FIRST, k * BLOCK, BLOCK, si1[0, k * n : (k + 1) * n], si1[1, k * n : (k + 1) * n])

    first_rows = halo_rows(xs1, FIRST, 0)
    start(first_rows)
    for p in range(3):
        for q in range(3):
            at = pl.ds((p * 3 + q) * channels, channels)
            w2[at, 0:channels] = k2[at, :]
            w2[at, channels : 2 * channels] = k2[pl.ds((q * 3 + p) * channels, channels), :]
    finish_rows(first_rows, xs1, FIRST)

    def mirror_copy(k):
        cut = pl.ds(k * BLOCK, BLOCK)
        return pltpu.make_async_remote_copy(
            h.at[:, cut], mir.at[:, cut], mir_send.at[k], mir_recv.at[k],
            device_id=mirror, device_id_type=MESH)

    def local_copy(k):
        cut = pl.ds(k * BLOCK, BLOCK)
        return pltpu.make_async_copy(h.at[:, cut], mir.at[:, cut], mir_send.at[k])

    for k in order:
        cut = slice(k * BLOCK, (k + 1) * BLOCK)

        @pl.loop(0, extent // BLOCK)
        def _(step):
            row = step * BLOCK
            taps = [
                xs1[q, pl.ds(row + p * FIRST, BLOCK), cut, :].reshape(BLOCK * BLOCK, channels)
                for p in range(3)
                for q in range(3)
            ]
            total = jnp.dot(jnp.concatenate(taps, axis=1), k1[...], preferred_element_type=jnp.float32)
            acted = jnp.maximum(total + b1[...], 0.0).astype(jnp.bfloat16)
            mixed = jnp.dot(acted, m1[...], preferred_element_type=jnp.float32) + s1[...]
            summed = (taps[4].astype(jnp.float32) + mixed).astype(jnp.bfloat16)
            h[pl.ds(row, BLOCK), cut, :] = summed.reshape(BLOCK, BLOCK, channels)

        @pl.when(off)
        def _():
            mirror_copy(k).start()

        @pl.when(jnp.logical_not(off))
        def _():
            local_copy(k).start()

    second_rows = halo_rows(xs2, SECOND, 1)

    def finish_chunk(k):
        copies = strips(so2.at[k], si2.at[k], 1 + k)
        finish_strips(copies, si2.at[k])
        patch(xs2, SECOND, k * BLOCK, BLOCK, si2[k, 0], si2[k, 1])
        if k == 0:
            start(second_rows[:1])
        if k == chunks - 1:
            start(second_rows[1:])

    for n, k in enumerate(order):
        cut = slice(k * BLOCK, (k + 1) * BLOCK)

        @pl.when(off)
        def _():
            mirror_copy(k).wait()

        @pl.when(jnp.logical_not(off))
        def _():
            local_copy(k).wait()

        flip[...] = mir[:, cut, :].astype(jnp.float32).reshape(extent * BLOCK, channels)
        for b in range(BLOCK):
            other = flip[pl.ds(b, extent, stride=BLOCK), :]
            row = k * BLOCK + b
            mean = jnp.maximum((h[row].astype(jnp.float32) + other) * 0.5, 0.0)
            spread_rows(xs2, SECOND, pl.ds(SECOND + row, 1), mean.reshape(1, extent, channels))
        at = pl.ds(SECOND + k * BLOCK, BLOCK)
        so2[k, 0] = pack(xs2[1, at, 0:16, :].astype(jnp.float32)[:, 0:8], 0, SECOND)
        so2[k, 1] = pack(
            xs2[1, at, extent - 16 : extent, :].astype(jnp.float32)[:, 8:16], 8 - SECOND, SECOND)
        start(strips(so2.at[k], si2.at[k], 1 + k))
        if n:
            finish_chunk(order[n - 1])
    finish_chunk(order[-1])
    finish_rows(second_rows, xs2, SECOND)

    group = 4

    @pl.loop(0, extent // group)
    def _(step):
        row = step * group
        taps = [
            xs2[q, pl.ds(row + p * SECOND, group)].reshape(group * extent, channels)
            for p in range(3)
            for q in range(3)
        ]
        total = jnp.dot(jnp.concatenate(taps, axis=1), w2[...], preferred_element_type=jnp.float32)
        center = taps[4].astype(jnp.float32)
        halves = []
        for side in range(2):
            part = total[:, side * channels : (side + 1) * channels]
            acted = jnp.maximum(part + b2[...], 0.0).astype(jnp.bfloat16)
            mixed = jnp.dot(acted, m2[...], preferred_element_type=jnp.float32) + s2[...]
            halves.append((center + mixed).astype(jnp.bfloat16).astype(jnp.float32))
        mean = jnp.maximum((halves[0] + halves[1]) * 0.5, 0.0)
        out[pl.ds(row, group)] = mean.reshape(group, extent, channels)


def body(
    features,
    kernel_first,
    bias_first,
    mixer_first,
    shift_first,
    kernel_second,
    bias_second,
    mixer_second,
    shift_second,
):
    extent, _, channels = features.shape
    chunks = extent // BLOCK
    bf16 = jnp.bfloat16
    cells = extent * extent
    vmem = pl.BlockSpec(memory_space=pltpu.VMEM)
    return pl.pallas_call(
        kernel,
        out_shape=jax.ShapeDtypeStruct(features.shape, jnp.float32),
        in_specs=[vmem] * 9,
        out_specs=vmem,
        scratch_shapes=[
            pltpu.VMEM((3, extent + 2 * FIRST, extent, channels), bf16),
            pltpu.VMEM((3, extent + 2 * SECOND, extent, channels), bf16),
            pltpu.VMEM((extent, extent, channels), bf16),
            pltpu.VMEM((extent, extent, channels), bf16),
            pltpu.VMEM((extent * BLOCK, channels), jnp.float32),
            pltpu.VMEM((9 * channels, 2 * channels), bf16),
            pltpu.VMEM((2, extent * FIRST, channels), bf16),
            pltpu.VMEM((2, extent * FIRST, channels), bf16),
            pltpu.VMEM((chunks, 2, BLOCK * SECOND, channels), bf16),
            pltpu.VMEM((chunks, 2, BLOCK * SECOND, channels), bf16),
            pltpu.SemaphoreType.DMA((1 + chunks, 2)),
            pltpu.SemaphoreType.DMA((1 + chunks, 2)),
            pltpu.SemaphoreType.DMA((2, 2)),
            pltpu.SemaphoreType.DMA((2, 2)),
            pltpu.SemaphoreType.DMA((chunks,)),
            pltpu.SemaphoreType.DMA((chunks,)),
        ],
        compiler_params=pltpu.CompilerParams(
            collective_id=0, has_side_effects=True, vmem_limit_bytes=40 * 1024 * 1024
        ),
        cost_estimate=pl.CostEstimate(
            flops=2 * cells * channels * channels * 30,
            bytes_accessed=cells * channels * 6,
            transcendentals=0,
        ),
    )(
        features,
        kernel_first.reshape(9 * channels, channels),
        bias_first.reshape(1, channels),
        mixer_first,
        shift_first.reshape(1, channels),
        kernel_second.reshape(9 * channels, channels),
        bias_second.reshape(1, channels),
        mixer_second,
        shift_second.reshape(1, channels),
    )


def solution(mesh):
    return jax.shard_map(
        body,
        mesh=mesh,
        in_specs=(P(("groups", "row"), "col", None), P(), P(), P(), P(), P(), P(), P(), P()),
        out_specs=P(("groups", "row"), "col", None),
        check_vma=False,
    )
```

time: 158 us -> 78 us (0.49); the launches traced: 154 us -> 77.6 us
  Pallas kernels: 0 us -> 69 us
  blocking collectives: 59.8 us -> 0 us
  matrix products: 31.1 us -> 0 us
  starting transfers between devices: 22 us -> 0 us
  other arithmetic: 16.4 us -> 0 us
  local copies, waits for them, and re-layouts: 20.2 us -> 8.6 us
  waiting for transfers between devices: 4.42 us -> 0 us
    pallas_call x0 -> x1, Pallas kernels: none -> 69 us  [body(): pl.pallas_call(kernel, out_shape=jax.ShapeDtypeStruct(features.shape, jnp...]
    all_to_all x3 -> x0, blocking collectives: 59.8 us -> none  [the longest x1 26.2 us: mirror_tile(): lax.all_to_all(lax.all_to_all(stacked, 'row', split_axis=0, concat_axis=1...]
    dot_general x27 -> x0, matrix products: 31.1 us -> none  [the longest x24 19.3 us: residual_sum(): jnp.dot(window.reshape(extent * extent, channels), kernel[tap_row, tap_co...]
    ppermute x8 -> x0, starting transfers between devices: 22 us -> none  [the longest x4 12.9 us: with_halo(): lax.ppermute(tail, axis, [(i, (i + 1) % count) for i in range(ends)])]
    slice x14 -> x0, local copies, waits for them, and re-layouts: 13.8 us -> none  [the longest x11 12.9 us: residual_sum(): extended[tap_row * spread:tap_row * spread + extent, tap_col * spread:tap...]
    concatenate x4 -> x0, other arithmetic: 9.44 us -> none  [with_halo(): jnp.concatenate([lax.ppermute(tail, axis, [(i, (i + 1) % count) for i in...]
    ppermute x8 -> x0, waiting for transfers between devices: 4.42 us -> none  [the longest x4 4.35 us: with_halo(): lax.ppermute(head, axis, [((i + 1) % count, i) for i in range(ends)])]
    max x1 -> x0, other arithmetic: 4 us -> none  [run_block(): jax.nn.relu((summed.astype(jnp.float32) + mirrored.astype(jnp.float32)) *...]
  transfers between devices with their start and end apart: 8 -> 0, of which waited for: 4 -> 0; matrix products, arithmetic and copies ran while one was open for 4% -> 0% of each run, Pallas kernels for 0% -> 0%
where the time goes in v1:
time: 78 us; the launch traced here: 77.6 us
  Pallas kernels  69 us (88%)
  local copies, waits for them, and re-layouts  8.6 us (11%)
    pallas_call x1, Pallas kernels, body(): pl.pallas_call(kernel, out_shape=jax.ShapeDtypeStruct(features.shape, jnp...  69 us
    unnamed x19, local copies, waits for them, and re-layouts  8.6 us

profile of v1, /device:TPU:17, one launch (start us, length us, event | category | flops | bytes accessed | tf_op | source)
XLA Modules:
  0.0 77.6 jit_solution(3604180714748878965)
XLA Ops:
  0.0 0.0 copy-start
  0.0 1.2 %copy-done = bf16[64,64,128]{2,1,0:T(8,128)(2,1)S(1)} copy-done((bf16[64,64,128]{2,1,0:T(8,128)(2,1)S(1)}, bf16[64,64,128]{2,1,0:T(8,128)(2,1)}, u32[]{:S(2)}) %copy-start) | copy-done | bytes 1048600
  1.2 0.0 copy-start.1
  1.2 1.0 %copy-done.1 = bf16[3,3,128,128]{3,2,1,0:T(8,128)(2,1)S(1)} copy-done((bf16[3,3,128,128]{3,2,1,0:T(8,128)(2,1)S(1)}, bf16[3,3,128,128]{3,2,1,0:T(8,128)(2,1)}, u32[]{:S(2)}) %copy-start.1) | copy-done | bytes 294936
  2.2 0.0 copy-start.2
  2.2 1.0 %copy-done.2 = bf16[3,3,128,128]{3,2,1,0:T(8,128)(2,1)S(1)} copy-done((bf16[3,3,128,128]{3,2,1,0:T(8,128)(2,1)S(1)}, bf16[3,3,128,128]{3,2,1,0:T(8,128)(2,1)}, u32[]{:S(2)}) %copy-start.2) | copy-done | bytes 294936
  3.1 0.0 copy-start.3
  3.2 0.8 copy-done.3
  3.9 0.0 copy-start.4
  3.9 0.8 copy-done.4
  4.7 0.0 copy-start.5
  4.7 0.7 copy-done.5
  5.3 0.0 copy-start.6
  5.3 0.7 copy-done.6
  6.0 0.0 copy-start.7
  6.0 0.7 copy-done.7
  6.6 0.0 copy-start.8
  6.6 0.7 copy-done.8
  7.3 69.0 %shard_map.91 = f32[64,64,128]{2,1,0:T(8,128)S(1)} custom-call(bf16[64,64,128]{2,1,0:T(8,128)(2,1)S(1)} %copy-done, bf16[1152,128]{1,0:T(8,128)(2,1)S(1)} %bitcast.6, f32[1,128]{1,0:T(1,128)S(1)} %bitcast.8, bf16[128,128]{1,0:T(8,128)(2,1)S(1)} %copy-done.3, f32[1,128]{1,0:T(1,128)S(1)} %bitcast.9, bf16[1152,128]{1,0:T(8,128)(2,1)S(1)} %bitcast.7, ...), custom_call_target="tpu_custom_call" | custom-call | flops 4026531840 | bytes 3145728 | tf_op jit(solution)/shard_map/pallas_call | solution.py:291
  76.3 1.3 %copy.11 = f32[64,64,128]{2,1,0:T(8,128)} copy(f32[64,64,128]{2,1,0:T(8,128)S(1)} %shard_map.91) | data formatting | bytes 4194304
Async XLA Ops:
  0.0 1.2 %copy-start = (bf16[64,64,128]{2,1,0:T(8,128)(2,1)S(1)}, bf16[64,64,128]{2,1,0:T(8,128)(2,1)}, u32[]{:S(2)}) copy-start(bf16[64,64,128]{2,1,0:T(8,128)(2,1)} %x.1) | copy-start | bytes 3145732
  1.2 1.0 %copy-start.1 = (bf16[3,3,128,128]{3,2,1,0:T(8,128)(2,1)S(1)}, bf16[3,3,128,128]{3,2,1,0:T(8,128)(2,1)}, u32[]{:S(2)}) copy-start(bf16[3,3,128,128]{3,2,1,0:T(8,128)(2,1)} %param.10) | copy-start | bytes 884740
  2.2 1.0 %copy-start.2 = (bf16[3,3,128,128]{3,2,1,0:T(8,128)(2,1)S(1)}, bf16[3,3,128,128]{3,2,1,0:T(8,128)(2,1)}, u32[]{:S(2)}) copy-start(bf16[3,3,128,128]{3,2,1,0:T(8,128)(2,1)} %param.14) | copy-start | bytes 884740
  3.1 0.8 copy-start.3
  3.9 0.8 copy-start.4
  4.7 0.7 copy-start.5
  5.3 0.7 copy-start.6
  6.0 0.7 copy-start.7
  6.6 0.7 copy-start.8

commit v2 on v1

--- a/solution.py
+++ b/solution.py
@@ -54,10 +54,17 @@
 
 
 def kernel(
-    x, k1, b1, m1, s1, k2, b2, m2, s2, out,
-    xs1, xs2, h, mir, flip, w2, so1, si1, so2, si2,
-    strip_send, strip_recv, rows_send, rows_recv, mir_send, mir_recv,
+    x_in, k1_in, b1_in, m1_in, s1_in, k2_in, b2_in, m2_in, s2_in, out_hbm,
+    x, k1, b1, m1, s1, k2, b2, m2, s2,
+    xs1, xs2, h, mir, flip, w2, so1, si1, so2, si2, relay, out,
+    load, strip_send, strip_recv, rows_send, rows_recv, mir_send, mir_recv,
+    relay_send, relay_recv, pass_send, out_sem,
 ):
+    held = (x, k1, b1, m1, s1, k2, b2, m2, s2)
+    given = (x_in, k1_in, b1_in, m1_in, s1_in, k2_in, b2_in, m2_in, s2_in)
+    loads = [pltpu.make_async_copy(a, b, load.at[n]) for n, (a, b) in enumerate(zip(given, held))]
+    for copy in loads:
+        copy.start()
     extent, _, channels = x.shape
     chunks = extent // BLOCK
     order = [0] + [chunks - 1] * (chunks > 1) + list(range(1, chunks - 1))
@@ -77,6 +84,28 @@
             pl.semaphore_signal(barrier, inc=1, device_id=peer, device_id_type=MESH)
     count = sum(has.astype(jnp.int32) for has, _ in peers)
 
+    on_diagonal = jnp.logical_not(off)
+
+    @pl.when(off)
+    def _():
+        pl.semaphore_signal(barrier, inc=1, device_id={"row": c}, device_id_type=MESH)
+        pl.semaphore_signal(barrier, inc=1, device_id={"col": r}, device_id_type=MESH)
+
+    def others(work):
+        @pl.loop(0, nr)
+        def _(other):
+            @pl.when(on_diagonal & (other != r))
+            def _():
+                work(other)
+
+    def greet(other):
+        pl.semaphore_signal(barrier, inc=1, device_id={"row": other}, device_id_type=MESH)
+        pl.semaphore_signal(barrier, inc=1, device_id={"col": other}, device_id_type=MESH)
+
+    others(greet)
+    count = count + jnp.where(off, 2, 2 * (nr - 1))
+    loads[0].wait()
+
     so1[0] = pack(x[:, 0:16, :].astype(jnp.float32)[:, 0:8], 0, FIRST)
     so1[1] = pack(x[:, extent - 16 : extent, :].astype(jnp.float32)[:, 8:16], 8 - FIRST, FIRST)
     pl.semaphore_wait(barrier, count)
@@ -170,6 +199,8 @@
 
     first_rows = halo_rows(xs1, FIRST, 0)
     start(first_rows)
+    for copy in loads[1:]:
+        copy.wait()
     for p in range(3):
         for q in range(3):
             at = pl.ds((p * 3 + q) * channels, channels)
@@ -177,17 +208,38 @@
             w2[at, channels : 2 * channels] = k2[pl.ds((q * 3 + p) * channels, channels), :]
     finish_rows(first_rows, xs1, FIRST)
 
+    half = extent // 2
+
     def mirror_copy(k):
         cut = pl.ds(k * BLOCK, BLOCK)
         return pltpu.make_async_remote_copy(
-            h.at[:, cut], mir.at[:, cut], mir_send.at[k], mir_recv.at[k],
+            h.at[0:half, cut], mir.at[0:half, cut], mir_send.at[k], mir_recv.at[0, k],
             device_id=mirror, device_id_type=MESH)
+
+    def relay_copy(k, source):
+        cut = pl.ds(k * BLOCK, BLOCK)
+        return pltpu.make_async_remote_copy(
+            h.at[half:extent, cut], relay.at[source, k], relay_send.at[k], relay_recv.at[source, k],
+            device_id={"row": c}, device_id_type=MESH)
+
+    def pass_copy(k, source):
+        cut = pl.ds(k * BLOCK, BLOCK)
+        return pltpu.make_async_remote_copy(
+            relay.at[source, k], mir.at[half:extent, cut], pass_send.at[source, k], mir_recv.at[1, k],
+            device_id={"col": source}, device_id_type=MESH)
+
+    def pass_chunk(k):
+        def work(source):
+            relay_copy(k, source).wait_recv()
+            pass_copy(k, source).start()
+
+        others(work)
 
     def local_copy(k):
         cut = pl.ds(k * BLOCK, BLOCK)
         return pltpu.make_async_copy(h.at[:, cut], mir.at[:, cut], mir_send.at[k])
 
-    for k in order:
+    for n, k in enumerate(order):
         cut = slice(k * BLOCK, (k + 1) * BLOCK)
 
         @pl.loop(0, extent // BLOCK)
@@ -207,53 +259,23 @@
         @pl.when(off)
         def _():
             mirror_copy(k).start()
-
-        @pl.when(jnp.logical_not(off))
+            relay_copy(k, r).start()
+
+        @pl.when(on_diagonal)
         def _():
             local_copy(k).start()
 
-    second_rows = halo_rows(xs2, SECOND, 1)
-
-    def finish_chunk(k):
-        copies = strips(so2.at[k], si2.at[k], 1 + k)
-        finish_strips(copies, si2.at[k])
-        patch(xs2, SECOND, k * BLOCK, BLOCK, si2[k, 0], si2[k, 1])
-        if k == 0:
-            start(second_rows[:1])
-        if k == chunks - 1:
-            start(second_rows[1:])
-
-    for n, k in enumerate(order):
-        cut = slice(k * BLOCK, (k + 1) * BLOCK)
-
-        @pl.when(off)
-        def _():
-            mirror_copy(k).wait()
-
-        @pl.when(jnp.logical_not(off))
-        def _():
-            local_copy(k).wait()
-
-        flip[...] = mir[:, cut, :].astype(jnp.float32).reshape(extent * BLOCK, channels)
-        for b in range(BLOCK):
-            other = flip[pl.ds(b, extent, stride=BLOCK), :]
-            row = k * BLOCK + b
-            mean = jnp.maximum((h[row].astype(jnp.float32) + other) * 0.5, 0.0)
-            spread_rows(xs2, SECOND, pl.ds(SECOND + row, 1), mean.reshape(1, extent, channels))
-        at = pl.ds(SECOND + k * BLOCK, BLOCK)
-        so2[k, 0] = pack(xs2[1, at, 0:16, :].astype(jnp.float32)[:, 0:8], 0, SECOND)
-        so2[k, 1] = pack(
-            xs2[1, at, extent - 16 : extent, :].astype(jnp.float32)[:, 8:16], 8 - SECOND, SECOND)
-        start(strips(so2.at[k], si2.at[k], 1 + k))
         if n:
-            finish_chunk(order[n - 1])
-    finish_chunk(order[-1])
-    finish_rows(second_rows, xs2, SECOND)
+            pass_chunk(order[n - 1])
+    pass_chunk(order[-1])
 
     group = 4
 
-    @pl.loop(0, extent // group)
-    def _(step):
+    def out_copy(step):
+        at = pl.ds(step * group, group)
+        return pltpu.make_async_copy(out.at[at], out_hbm.at[at], out_sem.at[step])
+
+    def second(step):
         row = step * group
         taps = [
             xs2[q, pl.ds(row + p * SECOND, group)].reshape(group * extent, channels)
@@ -270,6 +292,81 @@
             halves.append((center + mixed).astype(jnp.bfloat16).astype(jnp.float32))
         mean = jnp.maximum((halves[0] + halves[1]) * 0.5, 0.0)
         out[pl.ds(row, group)] = mean.reshape(group, extent, channels)
+        out_copy(step).start()
+
+    def second_range(steps):
+        steps = sorted(steps)
+        while steps:
+            n = 1
+            while n < len(steps) and steps[n] == steps[0] + n:
+                n += 1
+            pl.loop(steps[0], steps[0] + n)(second)
+            steps = steps[n:]
+
+    def needs(step):
+        lo, hi = step * group - SECOND, step * group + group + SECOND - 1
+        return {-1 if at < 0 or at >= extent else at // BLOCK for at in (lo, hi)}
+
+    waiting = set(range(extent // group))
+    ready = set()
+    done = set()
+
+    second_rows = halo_rows(xs2, SECOND, 1)
+
+    def finish_chunk(k):
+        copies = strips(so2.at[k], si2.at[k], 1 + k)
+        finish_strips(copies, si2.at[k])
+        patch(xs2, SECOND, k * BLOCK, BLOCK, si2[k, 0], si2[k, 1])
+        if k == 0:
+            start(second_rows[:1])
+        if k == chunks - 1:
+            start(second_rows[1:])
+
+    for n, k in enumerate(order):
+        cut = slice(k * BLOCK, (k + 1) * BLOCK)
+
+        @pl.when(off)
+        def _():
+            mirror_copy(k).wait()
+            relay_copy(k, r).wait_send()
+            pass_copy(k, r).wait_recv()
+
+        @pl.when(on_diagonal)
+        def _():
+            local_copy(k).wait()
+
+        flip[...] = mir[:, cut, :].astype(jnp.float32).reshape(extent * BLOCK, channels)
+        for b in range(BLOCK):
+            other = flip[pl.ds(b, extent, stride=BLOCK), :]
+            row = k * BLOCK + b
+            mean = jnp.maximum((h[row].astype(jnp.float32) + other) * 0.5, 0.0)
+            spread_rows(xs2, SECOND, pl.ds(SECOND + row, 1), mean.reshape(1, extent, channels))
+        at = pl.ds(SECOND + k * BLOCK, BLOCK)
+        so2[k, 0] = pack(xs2[1, at, 0:16, :].astype(jnp.float32)[:, 0:8], 0, SECOND)
+        so2[k, 1] = pack(
+            xs2[1, at, extent - 16 : extent, :].astype(jnp.float32)[:, 8:16], 8 - SECOND, SECOND)
+        start(strips(so2.at[k], si2.at[k], 1 + k))
+        second_range(ready)
+        finish_chunk(k)
+        done.add(k)
+        if n == min(1, chunks - 1):
+            finish_rows(second_rows, xs2, SECOND)
+            done.add(-1)
+        ready = {step for step in waiting if needs(step) <= done}
+        waiting -= ready
+        kept = set(sorted(ready)[-3:]) if n == chunks - 2 else set()
+        second_range(ready - kept)
+        ready = kept
+
+    def drain(source):
+        for k in range(chunks):
+            pass_copy(k, source).wait_send()
+
+    others(drain)
+
+    @pl.loop(0, extent // group)
+    def _(step):
+        out_copy(step).wait()
 
 
 def body(
@@ -285,15 +382,24 @@
 ):
     extent, _, channels = features.shape
     chunks = extent // BLOCK
+    side = lax.axis_size("row")
     bf16 = jnp.bfloat16
     cells = extent * extent
-    vmem = pl.BlockSpec(memory_space=pltpu.VMEM)
     return pl.pallas_call(
         kernel,
         out_shape=jax.ShapeDtypeStruct(features.shape, jnp.float32),
-        in_specs=[vmem] * 9,
-        out_specs=vmem,
+        in_specs=[pl.BlockSpec(memory_space=pltpu.HBM)] * 9,
+        out_specs=pl.BlockSpec(memory_space=pltpu.HBM),
         scratch_shapes=[
+            pltpu.VMEM((extent, extent, channels), bf16),
+            pltpu.VMEM((9 * channels, channels), bf16),
+            pltpu.VMEM((1, channels), jnp.float32),
+            pltpu.VMEM((channels, channels), bf16),
+            pltpu.VMEM((1, channels), jnp.float32),
+            pltpu.VMEM((9 * channels, channels), bf16),
+            pltpu.VMEM((1, channels), jnp.float32),
+            pltpu.VMEM((channels, channels), bf16),
+            pltpu.VMEM((1, channels), jnp.float32),
             pltpu.VMEM((3, extent + 2 * FIRST, extent, channels), bf16),
             pltpu.VMEM((3, extent + 2 * SECOND, extent, channels), bf16),
             pltpu.VMEM((extent, extent, channels), bf16),
@@ -304,15 +410,22 @@
             pltpu.VMEM((2, extent * FIRST, channels), bf16),
             pltpu.VMEM((chunks, 2, BLOCK * SECOND, channels), bf16),
             pltpu.VMEM((chunks, 2, BLOCK * SECOND, channels), bf16),
+            pltpu.VMEM((side, chunks, extent // 2, BLOCK, channels), bf16),
+            pltpu.VMEM((extent, extent, channels), jnp.float32),
+            pltpu.SemaphoreType.DMA((9,)),
             pltpu.SemaphoreType.DMA((1 + chunks, 2)),
             pltpu.SemaphoreType.DMA((1 + chunks, 2)),
             pltpu.SemaphoreType.DMA((2, 2)),
             pltpu.SemaphoreType.DMA((2, 2)),
             pltpu.SemaphoreType.DMA((chunks,)),
+            pltpu.SemaphoreType.DMA((2, chunks)),
             pltpu.SemaphoreType.DMA((chunks,)),
+            pltpu.SemaphoreType.DMA((side, chunks)),
+            pltpu.SemaphoreType.DMA((side, chunks)),
+            pltpu.SemaphoreType.DMA((extent // 4,)),
         ],
         compiler_params=pltpu.CompilerParams(
-            collective_id=0, has_side_effects=True, vmem_limit_bytes=40 * 1024 * 1024
+            collective_id=0, has_side_effects=True, vmem_limit_bytes=60 * 1024 * 1024
         ),
         cost_estimate=pl.CostEstimate(
             flops=2 * cells * channels * channels * 30,

time: 78 us -> 63.6 us (0.82)
  the two profiles are of different devices: /device:TPU:17 before, /device:TPU:10 now
where the time goes in v2:
time: 63.6 us; the launch traced here: 63.4 us
  Pallas kernels  60.2 us (95%)
  local copies, waits for them, and re-layouts  3.16 us (5%)
    pallas_call x1, Pallas kernels, body(): pl.pallas_call(kernel, out_shape=jax.ShapeDtypeStruct(features.shape, jnp...  60.2 us
    unnamed x1, local copies, waits for them, and re-layouts  3.16 us

profile of v2, /device:TPU:10, one launch (start us, length us, event | category | flops | bytes accessed | tf_op | source)
XLA Modules:
  0.0 63.4 jit_solution(11074846289485004937)
XLA Ops:
  0.0 60.2 %shard_map.91 = f32[64,64,128]{2,1,0:T(8,128)} custom-call(bf16[64,64,128]{2,1,0:T(8,128)(2,1)} %x_in.1, bf16[1152,128]{1,0:T(8,128)(2,1)} %bitcast.6, f32[1,128]{1,0:T(1,128)} %bitcast.8, bf16[128,128]{1,0:T(8,128)(2,1)} %m1_in.1, f32[1,128]{1,0:T(1,128)} %bitcast.9, bf16[1152,128]{1,0:T(8,128)(2,1)} %bitcast.7, f32[1,128]{1,0:T(1,128)} %bitcast.10, ...), custom_call_target="tpu_custom_call" | custom-call | flops 4026531840 | bytes 3145728 | tf_op jit(solution)/shard_map/pallas_call | solution.py:388
  60.2 3.2 %copy.11 = f32[64,64,128]{2,1,0:T(8,128)} copy(f32[64,64,128]{2,1,0:T(8,128)} %shard_map.91) | data formatting | bytes 4194304

commit v3 on v2

--- a/solution.py
+++ b/solution.py
@@ -239,14 +239,25 @@
         cut = pl.ds(k * BLOCK, BLOCK)
         return pltpu.make_async_copy(h.at[:, cut], mir.at[:, cut], mir_send.at[k])
 
+    def send_chunk(k):
+        @pl.when(off)
+        def _():
+            mirror_copy(k).start()
+            relay_copy(k, r).start()
+
+        @pl.when(on_diagonal)
+        def _():
+            local_copy(k).start()
+
+    tall = 2 * BLOCK
     for n, k in enumerate(order):
         cut = slice(k * BLOCK, (k + 1) * BLOCK)
 
-        @pl.loop(0, extent // BLOCK)
+        @pl.loop(0, extent // tall)
         def _(step):
-            row = step * BLOCK
+            row = step * tall
             taps = [
-                xs1[q, pl.ds(row + p * FIRST, BLOCK), cut, :].reshape(BLOCK * BLOCK, channels)
+                xs1[q, pl.ds(row + p * FIRST, tall), cut, :].reshape(tall * BLOCK, channels)
                 for p in range(3)
                 for q in range(3)
             ]
@@ -254,22 +265,14 @@
             acted = jnp.maximum(total + b1[...], 0.0).astype(jnp.bfloat16)
             mixed = jnp.dot(acted, m1[...], preferred_element_type=jnp.float32) + s1[...]
             summed = (taps[4].astype(jnp.float32) + mixed).astype(jnp.bfloat16)
-            h[pl.ds(row, BLOCK), cut, :] = summed.reshape(BLOCK, BLOCK, channels)
-
-        @pl.when(off)
-        def _():
-            mirror_copy(k).start()
-            relay_copy(k, r).start()
-
-        @pl.when(on_diagonal)
-        def _():
-            local_copy(k).start()
-
+            h[pl.ds(row, tall), cut, :] = summed.reshape(tall, BLOCK, channels)
+
+        if n < chunks - 1:
+            send_chunk(k)
         if n:
             pass_chunk(order[n - 1])
-    pass_chunk(order[-1])
-
-    group = 4
+
+    group = 8
 
     def out_copy(step):
         at = pl.ds(step * group, group)
@@ -308,7 +311,6 @@
         return {-1 if at < 0 or at >= extent else at // BLOCK for at in (lo, hi)}
 
     waiting = set(range(extent // group))
-    ready = set()
     done = set()
 
     second_rows = halo_rows(xs2, SECOND, 1)
@@ -346,17 +348,20 @@
         so2[k, 1] = pack(
             xs2[1, at, extent - 16 : extent, :].astype(jnp.float32)[:, 8:16], 8 - SECOND, SECOND)
         start(strips(so2.at[k], si2.at[k], 1 + k))
-        second_range(ready)
-        finish_chunk(k)
-        done.add(k)
-        if n == min(1, chunks - 1):
+        if n == chunks - 2:
+            send_chunk(order[-1])
+            pass_chunk(order[-1])
+            for other in order[:-1]:
+                finish_chunk(other)
             finish_rows(second_rows, xs2, SECOND)
-            done.add(-1)
-        ready = {step for step in waiting if needs(step) <= done}
-        waiting -= ready
-        kept = set(sorted(ready)[-3:]) if n == chunks - 2 else set()
-        second_range(ready - kept)
-        ready = kept
+            done |= {-1, *order[:-1]}
+            ready = {step for step in waiting if needs(step) <= done}
+            waiting -= ready
+            kept = set(sorted(ready)[-2:])
+            second_range(ready - kept)
+    second_range(kept)
+    finish_chunk(order[-1])
+    second_range(waiting)
 
     def drain(source):
         for k in range(chunks):
@@ -422,7 +427,7 @@
             pltpu.SemaphoreType.DMA((chunks,)),
             pltpu.SemaphoreType.DMA((side, chunks)),
             pltpu.SemaphoreType.DMA((side, chunks)),
-            pltpu.SemaphoreType.DMA((extent // 4,)),
+            pltpu.SemaphoreType.DMA((extent // 8,)),
         ],
         compiler_params=pltpu.CompilerParams(
             collective_id=0, has_side_effects=True, vmem_limit_bytes=60 * 1024 * 1024

time: 63.6 us -> 54 us (0.85)
  the two profiles are of different devices: /device:TPU:10 before, /device:TPU:17 now
where the time goes in v3:
time: 54 us; the launch traced here: 53.9 us
  Pallas kernels  50.7 us (94%)
  local copies, waits for them, and re-layouts  3.16 us (6%)
    pallas_call x1, Pallas kernels, body(): pl.pallas_call(kernel, out_shape=jax.ShapeDtypeStruct(features.shape, jnp...  50.7 us
    unnamed x1, local copies, waits for them, and re-layouts  3.16 us

profile of v3, /device:TPU:17, one launch (start us, length us, event | category | flops | bytes accessed | tf_op | source)
XLA Modules:
  0.0 53.9 jit_solution(17866812657563442476)
XLA Ops:
  0.0 50.7 %shard_map.91 = f32[64,64,128]{2,1,0:T(8,128)} custom-call(bf16[64,64,128]{2,1,0:T(8,128)(2,1)} %x_in.1, bf16[1152,128]{1,0:T(8,128)(2,1)} %bitcast.6, f32[1,128]{1,0:T(1,128)} %bitcast.8, bf16[128,128]{1,0:T(8,128)(2,1)} %m1_in.1, f32[1,128]{1,0:T(1,128)} %bitcast.9, bf16[1152,128]{1,0:T(8,128)(2,1)} %bitcast.7, f32[1,128]{1,0:T(1,128)} %bitcast.10, ...), custom_call_target="tpu_custom_call" | custom-call | flops 4026531840 | bytes 3145728 | tf_op jit(solution)/shard_map/pallas_call | solution.py:393
  50.7 3.2 %copy.11 = f32[64,64,128]{2,1,0:T(8,128)} copy(f32[64,64,128]{2,1,0:T(8,128)} %shard_map.91) | data formatting | bytes 4194304

commit v4 on v3

--- a/solution.py
+++ b/solution.py
@@ -206,6 +206,23 @@
             at = pl.ds((p * 3 + q) * channels, channels)
             w2[at, 0:channels] = k2[at, :]
             w2[at, channels : 2 * channels] = k2[pl.ds((q * 3 + p) * channels, channels), :]
+
+    def sums(row, tall, cut):
+        taps = [
+            xs1[q, pl.ds(row + p * FIRST, tall), cut, :].reshape(tall * BLOCK, channels)
+            for p in range(3)
+            for q in range(3)
+        ]
+        total = jnp.dot(jnp.concatenate(taps, axis=1), k1[...], preferred_element_type=jnp.float32)
+        acted = jnp.maximum(total + b1[...], 0.0).astype(jnp.bfloat16)
+        mixed = jnp.dot(acted, m1[...], preferred_element_type=jnp.float32) + s1[...]
+        summed = (taps[4].astype(jnp.float32) + mixed).astype(jnp.bfloat16)
+        h[pl.ds(row, tall), cut, :] = summed.reshape(tall, BLOCK, channels)
+
+    @pl.loop(0, extent // BLOCK - 2, step=2)
+    def _(step):
+        sums((step + 1) * BLOCK, 2 * BLOCK, slice(0, BLOCK))
+
     finish_rows(first_rows, xs1, FIRST)
 
     half = extent // 2
@@ -249,23 +266,16 @@
         def _():
             local_copy(k).start()
 
-    tall = 2 * BLOCK
     for n, k in enumerate(order):
         cut = slice(k * BLOCK, (k + 1) * BLOCK)
 
-        @pl.loop(0, extent // tall)
-        def _(step):
-            row = step * tall
-            taps = [
-                xs1[q, pl.ds(row + p * FIRST, tall), cut, :].reshape(tall * BLOCK, channels)
-                for p in range(3)
-                for q in range(3)
-            ]
-            total = jnp.dot(jnp.concatenate(taps, axis=1), k1[...], preferred_element_type=jnp.float32)
-            acted = jnp.maximum(total + b1[...], 0.0).astype(jnp.bfloat16)
-            mixed = jnp.dot(acted, m1[...], preferred_element_type=jnp.float32) + s1[...]
-            summed = (taps[4].astype(jnp.float32) + mixed).astype(jnp.bfloat16)
-            h[pl.ds(row, tall), cut, :] = summed.reshape(tall, BLOCK, channels)
+        if n:
+            @pl.loop(0, extent // (2 * BLOCK))
+            def _(step):
+                sums(step * 2 * BLOCK, 2 * BLOCK, cut)
+        else:
+            sums(0, BLOCK, cut)
+            sums(extent - BLOCK, BLOCK, cut)
 
         if n < chunks - 1:
             send_chunk(k)

time: 54 us -> 53.7 us (level)
  no operation moved by 1% of the time
where the time goes in v4:
time: 53.7 us; the launch traced here: 53.5 us
  Pallas kernels  50.3 us (94%)
  local copies, waits for them, and re-layouts  3.16 us (6%)
    pallas_call x1, Pallas kernels, body(): pl.pallas_call(kernel, out_shape=jax.ShapeDtypeStruct(features.shape, jnp...  50.3 us
    unnamed x1, local copies, waits for them, and re-layouts  3.16 us

profile of v4, /device:TPU:17, one launch (start us, length us, event | category | flops | bytes accessed | tf_op | source)
XLA Modules:
  0.0 53.5 jit_solution(16196565616124857108)
XLA Ops:
  0.0 50.3 %shard_map.91 = f32[64,64,128]{2,1,0:T(8,128)} custom-call(bf16[64,64,128]{2,1,0:T(8,128)(2,1)} %x_in.1, bf16[1152,128]{1,0:T(8,128)(2,1)} %bitcast.6, f32[1,128]{1,0:T(1,128)} %bitcast.8, bf16[128,128]{1,0:T(8,128)(2,1)} %m1_in.1, f32[1,128]{1,0:T(1,128)} %bitcast.9, bf16[1152,128]{1,0:T(8,128)(2,1)} %bitcast.7, f32[1,128]{1,0:T(1,128)} %bitcast.10, ...), custom_call_target="tpu_custom_call" | custom-call | flops 4026531840 | bytes 3145728 | tf_op jit(solution)/shard_map/pallas_call | solution.py:403
  50.4 3.2 %copy.11 = f32[64,64,128]{2,1,0:T(8,128)} copy(f32[64,64,128]{2,1,0:T(8,128)} %shard_map.91) | data formatting | bytes 4194304
